TPU v7x, 32 devices: a whole 2x2x4 slice. The times are simulated.
32 devices in a mesh: seq: 8 (over z, x), chan: 4 (over y, core).
Axes of the slice: x: 2, y: 2, z: 4, core: 2. Of those that a mesh axis runs over, the one named last changes fastest.
Arguments:
- query_in: bfloat16 [1024, 512], P('seq', 'chan'), may hold values from -6 to 6
- key_in: bfloat16 [1024, 512], P('seq', 'chan'), may hold values from -6 to 6
- value_in: bfloat16 [1024, 512], P('seq', 'chan'), may hold values from -6 to 6
- short_taps: float32 [3, 7, 512], P(None, None, 'chan'), may hold values from -2 to 2
- long_filters: bfloat16 [32, 1024], P('chan'), may hold values from -1.1 to 1.1
- skip_gain: float32 [512], P('chan'), may hold values from -1 to 1
- cotangent: bfloat16 [1024, 512], P('seq', 'chan'), may hold values from -6 to 6
Outputs:
- block_out: bfloat16 [1024, 512], P('seq', 'chan')
- input_grads: bfloat16 [3, 1024, 512], P(None, 'seq', 'chan')
- tap_grads: float32 [3, 7, 512], P(None, None, 'chan')
- skip_grad: float32 [512], P('chan')
- filter_grad: float32 [32, 1024], P('chan')
All inputs are finite; a program needn't handle non-finite values.
Results may differ from a plain program's by a relative error of at most 0.0085.
Values may be sent and summed in bfloat16 or wider, within the bound.
No kernel may reach another device: no remote copies, remote signals or barrier semaphores. Data moves between devices by JAX's collectives and lax.ppermute only.
A program may use at most 128 MiB of HBM per device.

v0:
```python
import functools
import math

import jax
import jax.numpy as jnp
from jax import lax
from jax.experimental import pallas as pl
from jax.experimental.pallas import tpu as pltpu
from jax.sharding import PartitionSpec as P


def from_behind(value, axis, steps):
    count = lax.axis_size(axis)
    initial, last = (max(0, -steps), min(count, count - steps))
    return lax.ppermute(value, axis, [(source, source + steps) for source in range(initial, last)])


def short_forward(extended, weights, rows_here):
    margin = weights.shape[0] - 1
    running = jnp.zeros((rows_here, extended.shape[1]), jnp.float32)
    for offset in range(weights.shape[0]):
        running = (
            running + weights[offset] * extended[margin - offset : margin - offset + rows_here]
        )
    return running


def short_backward(extended, weights, rows_here):
    running = jnp.zeros((rows_here, extended.shape[1]), jnp.float32)
    for offset in range(weights.shape[0]):
        running = running + weights[offset] * extended[offset : offset + rows_here]
    return running


def tap_sums(grad_rows, extended, tap_count, rows_here):
    margin = tap_count - 1
    sums_list = []
    for offset in range(tap_count):
        sums_list.append(
            jnp.sum(grad_rows * extended[margin - offset : margin - offset + rows_here], axis=0)
        )
    return jnp.stack(sums_list)


def hankel(padded, lag_start, height, breadth, seq_total):
    span = height + breadth - 1
    window = lax.dynamic_slice_in_dim(padded, lag_start + seq_total, span, axis=1)
    tiled = jnp.tile(window, (1, height))
    tiled = jnp.pad(tiled, ((0, 0), (0, height)))
    return tiled.reshape(padded.shape[0], height, span + 1)[:, :, :breadth]


def causal_part(padded, source_rows, source_start, target_start, target_count, seq_total):
    breadth = source_rows.shape[0]
    matrix = hankel(
        padded, target_start - source_start - breadth + 1, target_count, breadth, seq_total
    )
    return jnp.einsum("gts,sgc->tgc", matrix, source_rows[::-1], preferred_element_type=jnp.float32)


def anti_part(padded, target_rows, target_start, source_start, source_count, seq_total):
    breadth = target_rows.shape[0]
    matrix = hankel(
        padded, target_start - source_start - source_count + 1, source_count, breadth, seq_total
    )
    return jnp.einsum("gab,bgc->agc", matrix, target_rows, preferred_element_type=jnp.float32)[::-1]


def lag_part(buffer, target_rows, source_rows, target_start, source_start, seq_total):
    height = target_rows.shape[0]
    breadth = source_rows.shape[0]
    groups = target_rows.shape[1]
    padded_source = jnp.pad(source_rows[::-1], ((0, height), (0, 0), (0, 0)))
    products = jnp.einsum(
        "tgc,sgc->gts", target_rows, padded_source, preferred_element_type=jnp.float32
    )
    full_width = height + breadth
    skewed = products.reshape(groups, height * full_width)[:, : height * (full_width - 1)]
    skewed = skewed.reshape(groups, height, full_width - 1)
    diagonal = jnp.sum(skewed, axis=1)
    position = target_start - source_start - breadth + 1 + seq_total
    current = lax.dynamic_slice_in_dim(buffer, position, full_width - 1, axis=1)
    return lax.dynamic_update_slice_in_dim(buffer, current + diagonal, position, axis=1)


def local(query_in, key_in, value_in, short_taps, long_filters, skip_gain, cotangent):
    tok_rows, chan_width = query_in.shape
    groups, seq_total = long_filters.shape
    members = chan_width // groups
    tap_count = short_taps.shape[1]
    margin = tap_count - 1
    device = lax.axis_index("seq")
    own_start = device * tok_rows
    rim_rows = jnp.stack(
        [query_in[tok_rows - margin :], key_in[tok_rows - margin :], value_in[tok_rows - margin :]]
    )
    before = from_behind(rim_rows, "seq", 1)
    streams = [query_in, key_in, value_in]
    extended = [
        jnp.concatenate([before[stream], streams[stream]]).astype(jnp.float32)
        for stream in range(3)
    ]
    query_short = short_forward(extended[0], short_taps[0], tok_rows)
    key_short = short_forward(extended[1], short_taps[1], tok_rows)
    value_short = short_forward(extended[2], short_taps[2], tok_rows)
    gating = (key_short * value_short).astype(jnp.bfloat16)
    relayed = (cotangent.astype(jnp.float32) * query_short).astype(jnp.bfloat16)
    gating_wide = gating.astype(jnp.float32)
    relayed_wide = relayed.astype(jnp.float32)
    gating_groups = gating.reshape(tok_rows, groups, members)
    relayed_groups = relayed.reshape(tok_rows, groups, members)
    padded = jnp.concatenate([jnp.zeros((groups, seq_total), jnp.bfloat16), long_filters], axis=1)
    lag_buffer = jnp.zeros((groups, 2 * seq_total), jnp.float32)
    zeros_out = jnp.zeros((tok_rows, groups, members), jnp.float32)

    def target_pair(distance):
        return distance < 0

    totals = (zeros_out, lag_buffer)
    shard_rows = lax.all_gather(gating, "seq", axis=0, tiled=True)
    piece_rows = shard_rows.shape[0]
    step_rows = min(piece_rows, tok_rows)
    pieces = shard_rows.reshape(piece_rows // step_rows, step_rows, groups, members)

    def forward_visit_block(carried, element):
        position, rows_block = element
        source_start = position * step_rows

        def forward_active(partial_value):
            output_part, buffer = partial_value
            output_part = output_part + causal_part(
                padded, rows_block, source_start, own_start, tok_rows, seq_total
            )
            distance = device - source_start // tok_rows
            buffer = lax.cond(
                target_pair(distance),
                lambda held: lag_part(
                    held, relayed_groups, rows_block, own_start, source_start, seq_total
                ),
                lambda held: held,
                buffer,
            )
            return (output_part, buffer)

        carried = lax.cond(
            source_start < own_start + tok_rows,
            forward_active,
            lambda partial_value: partial_value,
            carried,
        )
        return (carried, None)

    totals, ignored = lax.scan(
        forward_visit_block, totals, (jnp.arange(piece_rows // step_rows, dtype=jnp.int32), pieces)
    )
    output_part, lag_buffer = totals
    output_sum = output_part.reshape(tok_rows, chan_width)
    totals = (zeros_out, lag_buffer)
    shard_rows = lax.all_gather(relayed, "seq", axis=0, tiled=True)
    piece_rows = shard_rows.shape[0]
    backward_step_rows = min(piece_rows, tok_rows)
    pieces = shard_rows.reshape(
        piece_rows // backward_step_rows, backward_step_rows, groups, members
    )

    def backward_visit_block(carried, element):
        position, rows_block = element
        target_start = position * backward_step_rows

        def backward_active(partial_value):
            grad_part, buffer = partial_value
            grad_part = grad_part + anti_part(
                padded, rows_block, target_start, own_start, tok_rows, seq_total
            )
            distance = target_start // tok_rows - device
            buffer = lax.cond(
                target_pair(distance),
                lambda held: held,
                lambda held: lag_part(
                    held, rows_block, gating_groups, target_start, own_start, seq_total
                ),
                buffer,
            )
            return (grad_part, buffer)

        carried = lax.cond(
            target_start + backward_step_rows > own_start,
            backward_active,
            lambda partial_value: partial_value,
            carried,
        )
        return (carried, None)

    totals, ignored = lax.scan(
        backward_visit_block,
        totals,
        (jnp.arange(piece_rows // backward_step_rows, dtype=jnp.int32), pieces),
    )
    grad_part, lag_buffer = totals
    grad_sum = grad_part.reshape(tok_rows, chan_width)
    lag_local = lag_buffer[:, seq_total:]
    long_out = output_sum + skip_gain * gating_wide
    block_out = (query_short * long_out).astype(jnp.bfloat16)
    grad_gating = grad_sum + skip_gain * relayed_wide
    cot_wide = cotangent.astype(jnp.float32)
    grad_shorts = [cot_wide * long_out, grad_gating * value_short, grad_gating * key_short]
    lead_rows = jnp.stack([grad_shorts[stream][:margin] for stream in range(3)])
    after = from_behind(lead_rows, "seq", -1)
    input_grads = jnp.stack(
        [
            short_backward(
                jnp.concatenate([grad_shorts[stream], after[stream]]), short_taps[stream], tok_rows
            )
            for stream in range(3)
        ]
    ).astype(jnp.bfloat16)
    tap_local = jnp.stack(
        [
            tap_sums(grad_shorts[stream], extended[stream], tap_count, tok_rows)
            for stream in range(3)
        ]
    )
    skip_local = jnp.sum(relayed_wide * gating_wide, axis=0)
    lag_total, tap_total, skip_total = lax.psum((lag_local, tap_local, skip_local), "seq")
    tap_scale = 1.0 / math.sqrt(seq_total)
    lag_scale = 1.0 / math.sqrt(seq_total * members)
    return (
        block_out,
        input_grads,
        tap_total * tap_scale,
        skip_total * tap_scale,
        lag_total * lag_scale,
    )


def pack_kernel(
    query_ref, key_ref, value_ref, cot_ref, skip_ref, out_ref, gain_ref, stream_buf, sems
):
    count, streams, members, tok_rows = out_ref.shape
    moves = [
        pltpu.make_async_copy(ref, stream_buf.at[stream], sems.at[stream])
        for stream, ref in enumerate((query_ref, key_ref, value_ref, cot_ref))
    ]
    moves.append(pltpu.make_async_copy(skip_ref, gain_ref, sems.at[streams]))
    for move in moves:
        move.start()
    for stream in range(streams):
        moves[stream].wait()
        flipped = stream_buf[stream].astype(jnp.float32).T.astype(jnp.bfloat16)
        out_ref[:, stream] = flipped.reshape(count, members, tok_rows)
    moves[streams].wait()


def group_kernel(
    in_ref, taps_ref, filters_ref, gain_ref, out_ref, table_ref, wide_ref, tile_ref
):
    count, _, members, span = in_ref.shape
    groups, seq_total = filters_ref.shape
    streams, tap_count, chan_width = taps_ref.shape
    rows = count * members
    mine = lax.axis_index("seq")
    shape = (count, members, span)
    lane = lax.broadcasted_iota(jnp.int32, shape, 2)
    reach = 3

    def later(value, steps):
        if steps == 0:
            return value
        turned = pltpu.roll(value, steps, 2)
        before = jnp.concatenate([jnp.zeros_like(turned[:1]), turned[:-1]], axis=0)
        return jnp.where(lane >= steps, turned, before)

    def earlier(value, steps):
        if steps == 0:
            return value
        turned = pltpu.roll(value, span - steps, 2)
        after = jnp.concatenate([turned[1:], jnp.zeros_like(turned[:1])], axis=0)
        return jnp.where(lane < span - steps, turned, after)

    table = jnp.concatenate(
        [taps_ref[stream] for stream in range(streams)]
        + [gain_ref[...], jnp.zeros((2, chan_width), jnp.float32)],
        axis=0,
    )
    table_ref[...] = table.T
    params = table_ref[pl.ds(pl.multiple_of(mine * members, members), members), :]

    def column(index):
        return jnp.broadcast_to(params[:, index : index + 1], (members, span))[None]

    chosen = lax.broadcasted_iota(jnp.int32, (groups, 1), 0) == mine
    filter_row = jnp.sum(
        jnp.where(chosen, filters_ref[...].astype(jnp.float32), 0.0), axis=0, keepdims=True
    )
    filter_row = jnp.concatenate([filter_row, jnp.zeros((1, span), jnp.float32)], axis=1)
    spread = jnp.broadcast_to(filter_row, (members, seq_total + span))
    first_rows = pltpu.roll(spread, 0, 1, stride=1, stride_axis=0).astype(jnp.bfloat16)
    row_parts = [first_rows] + [
        pltpu.roll(first_rows, first, 1) for first in range(members, span, members)
    ]
    toeplitz = jnp.concatenate(row_parts, axis=0)[:, :seq_total]

    def delays(stream):
        return [later(in_ref[:, stream], first) for first in range(0, tap_count, reach)]

    def short(stream, values):
        total = None
        for second in range(reach):
            running = None
            for first in range(second, tap_count, reach):
                value = values[first // reach].astype(jnp.float32)
                term = column(stream * tap_count + first) * value
                running = term if running is None else running + term
            running = later(running, second)
            total = running if total is None else total + running
        return total

    def ahead_by_blocks(value):
        parts = [value]
        for step in range(1, count):
            gap = jnp.zeros((step * members, span), jnp.bfloat16)
            parts.append(jnp.concatenate([value[step * members :], gap], axis=0))
        return jnp.concatenate(parts, axis=1)

    gain = column(streams * tap_count)
    cot = in_ref[:, streams].astype(jnp.float32)
    delayed = [delays(0)]
    query_short = short(0, delayed[0])
    relayed = (cot * query_short).astype(jnp.bfloat16).reshape(rows, span)
    relayed_lags = ahead_by_blocks(relayed)
    backward = lax.dot_general(
        relayed_lags, toeplitz, (((1,), (1,)), ((), ())), preferred_element_type=jnp.float32
    )

    delayed += [delays(1), delays(2)]
    key_short = short(1, delayed[1])
    value_short = short(2, delayed[2])
    gating = (key_short * value_short).astype(jnp.bfloat16).reshape(rows, span)
    gating_parts, filter_parts = [gating], [toeplitz[:, :span]]
    for step in range(1, count):
        gap = jnp.zeros((step * members, span), jnp.bfloat16)
        gating_parts.append(jnp.concatenate([gap, gating[: rows - step * members]], axis=0))
        filter_parts.append(toeplitz[:, step * span : (step + 1) * span])
    forward = jnp.dot(
        jnp.concatenate(gating_parts, axis=1),
        jnp.concatenate(filter_parts, axis=0),
        preferred_element_type=jnp.float32,
    )

    half = span // 2
    flip = (
        lax.broadcasted_iota(jnp.int32, (span, span), 0)
        + lax.broadcasted_iota(jnp.int32, (span, span), 1)
        == span - 1
    ).astype(jnp.bfloat16)
    gating_turned = lax.dot_general(
        flip, gating, (((1,), (1,)), ((), ())), preferred_element_type=jnp.float32
    ).astype(jnp.bfloat16)
    gating_turned = jnp.concatenate([gating_turned[half:], gating_turned[:half]], axis=1)
    ahead = earlier(relayed.reshape(shape), half).reshape(rows, span)
    targets = jnp.concatenate([relayed_lags, ahead_by_blocks(ahead)], axis=0)
    wide_ref[:, :seq_total] = jnp.dot(
        gating_turned, targets, preferred_element_type=jnp.float32
    )
    wide_ref[:, seq_total:] = jnp.zeros((half, span), jnp.float32)

    tap_scale = 1.0 / math.sqrt(seq_total)

    def tokens(value):
        return jnp.concatenate([value[block] for block in range(count)], axis=1)

    def sums(left, right):
        product = lax.dot_general(
            jnp.concatenate(left, axis=0),
            jnp.concatenate(right, axis=0),
            (((1,), (1,)), ((), ())),
            preferred_element_type=jnp.float32,
        )
        same = (
            lax.broadcasted_iota(jnp.int32, product.shape, 0) % members
            == lax.broadcasted_iota(jnp.int32, product.shape, 1) % members
        )
        product = jnp.where(same, product, 0.0).reshape(len(left), members, -1)
        return jnp.sum(product, axis=1) * tap_scale

    tile_ref[...] = jnp.zeros((members, span), jnp.float32)

    def finish(stream, grad_short, first_row, more_left=(), more_right=()):
        moved = [earlier(grad_short, second) for second in range(reach)]
        left = [tokens(value.astype(jnp.bfloat16)) for value in moved] + list(more_left)
        right = [tokens(value) for value in delayed[stream]] + list(more_right)
        totals = sums(left, right)
        tile_ref[first_row : first_row + len(left), : totals.shape[1]] = totals
        total = None
        for place in range(len(delayed[stream])):
            running = None
            for second in range(min(reach, tap_count - reach * place)):
                term = column(stream * tap_count + reach * place + second) * moved[second]
                running = term if running is None else running + term
            running = earlier(running, reach * place)
            total = running if total is None else total + running
        out_ref[:, 1 + stream] = total.astype(jnp.bfloat16)

    grad_gating = backward.reshape(shape) + gain * relayed.astype(jnp.float32).reshape(shape)
    finish(1, grad_gating * value_short, reach + 1)
    finish(2, grad_gating * key_short, 2 * reach + 1)

    long_out = forward.reshape(shape) + gain * gating.astype(jnp.float32).reshape(shape)
    out_ref[:, 0] = (query_short * long_out).astype(jnp.bfloat16)
    finish(
        0, cot * long_out, 0, [tokens(relayed.reshape(shape))], [tokens(gating.reshape(shape))]
    )

    skewed = pltpu.roll(wide_ref[...], span - half + 1, 1, stride=1, stride_axis=0)
    diagonal = jnp.sum(skewed, axis=0, keepdims=True)
    lag_scale = 1.0 / math.sqrt(seq_total * members)
    lag_sums = jnp.concatenate(
        [diagonal[:, step * span : (step + 1) * span] for step in range(1, count + 1)], axis=0
    )
    lag_sums = lag_sums * lag_scale
    tile_ref[:count, half:] = lag_sums[:, half:]
    tile_ref[count:, half:] = pltpu.roll(lag_sums, half, 1)[:, half:]
    out_ref[:, streams + 1] = jnp.broadcast_to(tile_ref[...].astype(jnp.bfloat16)[None], shape)


def unpack_kernel(in_ref, out_ref, grads_ref, taps_ref, skip_ref, lags_ref):
    count, _, members, span = in_ref.shape
    streams, tap_count, chan_width = taps_ref.shape
    reach = 3
    for stream in range(streams + 1):
        block = in_ref[:, stream].reshape(count * members, span).astype(jnp.float32)
        flipped = block.T.astype(jnp.bfloat16)
        if stream == 0:
            out_ref[...] = flipped
        else:
            grads_ref[stream - 1] = flipped
    tile = in_ref[:, streams + 1].astype(jnp.float32)
    lane = lax.broadcasted_iota(jnp.int32, (1, members // 2, span), 2)
    lags = jnp.where(
        lane < span // 2, pltpu.roll(tile[:, members // 2 :], span // 2, 2), tile[:, : members // 2]
    )
    for step in range(members // 2):
        lags_ref[:, step * span : (step + 1) * span] = lags[:, step]
    lane = lax.broadcasted_iota(jnp.int32, (members, span), 1)
    spread = []
    for place in range(-(-tap_count // reach) + 1):
        total = None
        for group in range(count):
            moved = pltpu.roll(tile[group], (members * (group - place)) % span, 1)
            inside = (lane >= members * group) & (lane < members * (group + 1))
            total = moved if total is None else jnp.where(inside, moved, total)
        spread.append(total)
    first = 0
    for stream in range(streams):
        for place in range(-(-tap_count // reach)):
            taken = min(reach, tap_count - reach * place)
            taps_ref[stream, reach * place : reach * place + taken] = spread[place][
                first : first + taken
            ]
        first += reach + (stream == 0)
    skip_ref[...] = spread[-1][reach : reach + 1]


def by_group(query_in, key_in, value_in, short_taps, long_filters, skip_gain, cotangent):
    tok_rows, chan_width = query_in.shape
    groups, seq_total = long_filters.shape
    streams, tap_count, _ = short_taps.shape
    members = chan_width // groups
    count = groups
    vmem = pl.BlockSpec(memory_space=pltpu.VMEM)
    params = pltpu.CompilerParams(vmem_limit_bytes=32 * 1024 * 1024)
    packed, gain = pl.pallas_call(
        pack_kernel,
        out_shape=(
            jax.ShapeDtypeStruct((count, streams + 1, members, tok_rows), jnp.bfloat16),
            jax.ShapeDtypeStruct((1, chan_width), jnp.float32),
        ),
        in_specs=[pl.BlockSpec(memory_space=pltpu.HBM)] * 5,
        out_specs=(vmem,) * 2,
        scratch_shapes=[
            pltpu.VMEM((streams + 1, tok_rows, chan_width), jnp.bfloat16),
            pltpu.SemaphoreType.DMA((streams + 2,)),
        ],
        compiler_params=params,
        name="pack",
    )(
        *(
            pltpu.with_memory_space_constraint(value, pltpu.HBM)
            for value in (
                query_in, key_in, value_in, cotangent, skip_gain.reshape(1, chan_width)
            )
        )
    )
    packed = lax.all_to_all(packed, "seq", 0, 0, tiled=True)
    results = pl.pallas_call(
        group_kernel,
        out_shape=jax.ShapeDtypeStruct((count, streams + 2, members, tok_rows), jnp.bfloat16),
        in_specs=[vmem] * 4,
        out_specs=vmem,
        scratch_shapes=[
            pltpu.VMEM((chan_width, streams * tap_count + 3), jnp.float32),
            pltpu.VMEM((tok_rows // 2, seq_total + tok_rows), jnp.float32),
            pltpu.VMEM((members, tok_rows), jnp.float32),
        ],
        compiler_params=params,
        name="group",
    )(packed, short_taps, long_filters, gain)
    results = lax.all_to_all(results, "seq", 0, 0, tiled=True)
    block_out, input_grads, tap_grads, skip_grad, filter_grad = pl.pallas_call(
        unpack_kernel,
        out_shape=(
            jax.ShapeDtypeStruct((tok_rows, chan_width), jnp.bfloat16),
            jax.ShapeDtypeStruct((streams, tok_rows, chan_width), jnp.bfloat16),
            jax.ShapeDtypeStruct((streams, tap_count, chan_width), jnp.float32),
            jax.ShapeDtypeStruct((1, chan_width), jnp.float32),
            jax.ShapeDtypeStruct((groups, seq_total), jnp.float32),
        ),
        in_specs=[vmem],
        out_specs=(vmem,) * 5,
        compiler_params=params,
        name="unpack",
    )(results)
    return block_out, input_grads, tap_grads, skip_grad.reshape(chan_width), filter_grad


def plan(query_in, key_in, value_in, short_taps, long_filters, skip_gain, cotangent):
    tok_rows, chan_width = query_in.shape
    groups, seq_total = long_filters.shape
    fits = (
        lax.axis_size("seq") == groups
        and tok_rows == 128
        and chan_width == 128
        and chan_width // groups == 16
        and seq_total == groups * tok_rows
        and short_taps.shape[:2] == (3, 7)
    )
    chosen = by_group if fits else local
    return chosen(query_in, key_in, value_in, short_taps, long_filters, skip_gain, cotangent)


def solution(mesh):
    in_specs = (
        P("seq", "chan"),
        P("seq", "chan"),
        P("seq", "chan"),
        P(None, None, "chan"),
        P("chan", None),
        P("chan"),
        P("seq", "chan"),
    )
    out_specs = (
        P("seq", "chan"),
        P(None, "seq", "chan"),
        P(None, None, "chan"),
        P("chan"),
        P("chan", None),
    )
    return jax.shard_map(plan, mesh=mesh, in_specs=in_specs, out_specs=out_specs, check_vma=False)
```

profile of v0, /device:TPU:0, one launch (start us, length us, event | category | flops | bytes accessed | tf_op | source)
XLA Modules:
  0.0 28.1 jit_solution(3853962813884209661)
XLA Ops:
  0.6 1.2 %pack.1 = (bf16[8,4,16,128]{3,2,1,0:T(8,128)(2,1)S(1)}, f32[1,128]{1,0:T(1,128)S(1)}) custom-call(bf16[128,128]{1,0:T(8,128)(2,1)} %query_ref.1, bf16[128,128]{1,0:T(8,128)(2,1)} %key_ref.1, bf16[128,128]{1,0:T(8,128)(2,1)} %value_ref.1, bf16[128,128]{1,0:T(8,128)(2,1)} %cot_ref.1, f32[1,128]{1,0:T(1,128)} %bitcast.2), custom_call_target="tpu_custom_call" | custom-call | tf_op jit(solution)/shard_map/pack/pallas_call | solution.py:472
  1.9 0.0 copy-start
  1.9 0.0 copy-start.1
  1.9 14.4 %all_to_all.10.in_ref = bf16[8,4,16,128]{3,2,1,0:T(8,128)(2,1)S(1)} all-to-all(bf16[8,4,16,128]{3,2,1,0:T(8,128)(2,1)S(1)} %get-tuple-element.12), channel_id=1, replica_groups=mesh['seq'=8,'chan'=4] {'seq'}, dimensions={0} | all-to-all | bytes 262144 | tf_op jit(solution)/shard_map/all_to_all | solution.py:494
  16.3 0.0 copy-done
  16.3 0.0 copy-done.1
  16.3 1.1 %group.1 = bf16[8,5,16,128]{3,2,1,0:T(8,128)(2,1)S(1)} custom-call(bf16[8,4,16,128]{3,2,1,0:T(8,128)(2,1)S(1)} %all_to_all.10.in_ref, f32[3,7,128]{2,1,0:T(8,128)S(1)} %copy-done.1, bf16[8,1024]{1,0:T(8,128)(2,1)S(1)} %copy-done, f32[1,128]{1,0:T(1,128)S(1)} %get-tuple-element.13.gain_ref), custom_call_target="tpu_custom_call" | custom-call | tf_op jit(solution)/shard_map/group/pallas_call | solution.py:495
  17.4 10.0 %all_to_all.11.in_ref = bf16[8,5,16,128]{3,2,1,0:T(8,128)(2,1)S(1)} all-to-all(bf16[8,5,16,128]{3,2,1,0:T(8,128)(2,1)S(1)} %group.1), channel_id=1, replica_groups=mesh['seq'=8,'chan'=4] {'seq'}, dimensions={0} | all-to-all | bytes 327680 | tf_op jit(solution)/shard_map/all_to_all | solution.py:508
  27.3 0.8 %unpack.1 = (bf16[128,128]{1,0:T(8,128)(2,1)}, bf16[3,128,128]{2,1,0:T(8,128)(2,1)}, f32[3,7,128]{2,1,0:T(8,128)}, f32[1,128]{1,0:T(1,128)}, f32[8,1024]{1,0:T(8,128)}) custom-call(bf16[8,5,16,128]{3,2,1,0:T(8,128)(2,1)S(1)} %all_to_all.11.in_ref), custom_call_target="tpu_custom_call" | custom-call | tf_op jit(solution)/shard_map/unpack/pallas_call | solution.py:509
Async XLA Ops:
  1.9 14.4 %copy-start = (bf16[8,1024]{1,0:T(8,128)(2,1)S(1)}, bf16[8,1024]{1,0:T(8,128)(2,1)}, u32[]{:S(2)}) copy-start(bf16[8,1024]{1,0:T(8,128)(2,1)} %filters_ref.1) | copy-start | bytes 49156
  1.9 14.4 %copy-start.1 = (f32[3,7,128]{2,1,0:T(8,128)S(1)}, f32[3,7,128]{2,1,0:T(8,128)}, u32[]{:S(2)}) copy-start(f32[3,7,128]{2,1,0:T(8,128)} %taps_ref.1) | copy-start | bytes 32260
where the time goes:
time: 28.4 us; the launch traced here: 28.1 us
  blocking collectives  24.3 us (86%)
  Pallas kernels  3.1 us (11%)
  between operations  0.66 us (2%)
    all_to_all x1, blocking collectives, by_group(): packed = lax.all_to_all(packed, 'seq', 0, 0, tiled=True)  14.4 us
    all_to_all x1, blocking collectives, by_group(): results = lax.all_to_all(results, 'seq', 0, 0, tiled=True)  9.95 us
    pallas_call x1, Pallas kernels, by_group(): pl.pallas_call(pack_kernel, out_shape=(jax.ShapeDtypeStruct((count, strea...  1.22 us
    pallas_call x1, Pallas kernels, by_group(): pl.pallas_call(group_kernel, out_shape=jax.ShapeDtypeStruct((count, strea...  1.11 us
    pallas_call x1, Pallas kernels, by_group(): pl.pallas_call(unpack_kernel, out_shape=(jax.ShapeDtypeStruct((tok_rows,...  0.77 us

commit v1 on v0

--- a/solution.py
+++ b/solution.py
@@ -233,6 +233,19 @@
     )
 
 
+def member_order(count):
+    return list(range(count))[::-1]
+
+
+def in_order(value, count):
+    order = member_order(count)
+    return jnp.stack([value[order.index(device)] for device in range(count)])
+
+
+def by_member(value, count):
+    return jnp.stack([value[device] for device in member_order(count)])
+
+
 def pack_kernel(
     query_ref, key_ref, value_ref, cot_ref, skip_ref, out_ref, gain_ref, stream_buf, sems
 ):
@@ -247,7 +260,7 @@
     for stream in range(streams):
         moves[stream].wait()
         flipped = stream_buf[stream].astype(jnp.float32).T.astype(jnp.bfloat16)
-        out_ref[:, stream] = flipped.reshape(count, members, tok_rows)
+        out_ref[:, stream] = by_member(flipped.reshape(count, members, tok_rows), count)
     moves[streams].wait()
 
 
@@ -301,7 +314,8 @@
     toeplitz = jnp.concatenate(row_parts, axis=0)[:, :seq_total]
 
     def delays(stream):
-        return [later(in_ref[:, stream], first) for first in range(0, tap_count, reach)]
+        value = in_order(in_ref[:, stream], count)
+        return [later(value, first) for first in range(0, tap_count, reach)]
 
     def short(stream, values):
         total = None
@@ -323,7 +337,7 @@
         return jnp.concatenate(parts, axis=1)
 
     gain = column(streams * tap_count)
-    cot = in_ref[:, streams].astype(jnp.float32)
+    cot = in_order(in_ref[:, streams], count).astype(jnp.float32)
     delayed = [delays(0)]
     query_short = short(0, delayed[0])
     relayed = (cot * query_short).astype(jnp.bfloat16).reshape(rows, span)
@@ -399,14 +413,14 @@
                 running = term if running is None else running + term
             running = earlier(running, reach * place)
             total = running if total is None else total + running
-        out_ref[:, 1 + stream] = total.astype(jnp.bfloat16)
+        out_ref[:, 1 + stream] = by_member(total.astype(jnp.bfloat16), count)
 
     grad_gating = backward.reshape(shape) + gain * relayed.astype(jnp.float32).reshape(shape)
     finish(1, grad_gating * value_short, reach + 1)
     finish(2, grad_gating * key_short, 2 * reach + 1)
 
     long_out = forward.reshape(shape) + gain * gating.astype(jnp.float32).reshape(shape)
-    out_ref[:, 0] = (query_short * long_out).astype(jnp.bfloat16)
+    out_ref[:, 0] = by_member((query_short * long_out).astype(jnp.bfloat16), count)
     finish(
         0, cot * long_out, 0, [tokens(relayed.reshape(shape))], [tokens(gating.reshape(shape))]
     )
@@ -428,13 +442,14 @@
     streams, tap_count, chan_width = taps_ref.shape
     reach = 3
     for stream in range(streams + 1):
-        block = in_ref[:, stream].reshape(count * members, span).astype(jnp.float32)
+        block = in_order(in_ref[:, stream], count).reshape(count * members, span)
+        block = block.astype(jnp.float32)
         flipped = block.T.astype(jnp.bfloat16)
         if stream == 0:
             out_ref[...] = flipped
         else:
             grads_ref[stream - 1] = flipped
-    tile = in_ref[:, streams + 1].astype(jnp.float32)
+    tile = in_order(in_ref[:, streams + 1], count).astype(jnp.float32)
     lane = lax.broadcasted_iota(jnp.int32, (1, members // 2, span), 2)
     lags = jnp.where(
         lane < span // 2, pltpu.roll(tile[:, members // 2 :], span // 2, 2), tile[:, : members // 2]
@@ -491,7 +506,9 @@
             )
         )
     )
-    packed = lax.all_to_all(packed, "seq", 0, 0, tiled=True)
+    packed = lax.all_to_all(
+        packed, "seq", 0, 0, tiled=True, axis_index_groups=[member_order(count)]
+    )
     results = pl.pallas_call(
         group_kernel,
         out_shape=jax.ShapeDtypeStruct((count, streams + 2, members, tok_rows), jnp.bfloat16),
@@ -505,7 +522,9 @@
         compiler_params=params,
         name="group",
     )(packed, short_taps, long_filters, gain)
-    results = lax.all_to_all(results, "seq", 0, 0, tiled=True)
+    results = lax.all_to_all(
+        results, "seq", 0, 0, tiled=True, axis_index_groups=[member_order(count)]
+    )
     block_out, input_grads, tap_grads, skip_grad, filter_grad = pl.pallas_call(
         unpack_kernel,
         out_shape=(

time: 28.4 us -> 26.4 us (0.930)
  blocking collectives: 24.3 us -> 22.3 us
    all_to_all x2, blocking collectives: 24.3 us -> 22.3 us  [the longest x1 12.3 us: by_group(): lax.all_to_all(packed, 'seq', 0, 0, tiled=True, axis_index_groups=[member...]
where the time goes in v1:
time: 26.4 us; the launch traced here: 26.1 us
  blocking collectives  22.3 us (84%)
  Pallas kernels  3.1 us (12%)
  between operations  0.66 us (2%)
    all_to_all x1, blocking collectives, by_group(): lax.all_to_all(packed, 'seq', 0, 0, tiled=True, axis_index_groups=[member...  12.3 us
    all_to_all x1, blocking collectives, by_group(): lax.all_to_all(results, 'seq', 0, 0, tiled=True, axis_index_groups=[membe...  10 us
    pallas_call x1, Pallas kernels, by_group(): pl.pallas_call(pack_kernel, out_shape=(jax.ShapeDtypeStruct((count, strea...  1.22 us
    pallas_call x1, Pallas kernels, by_group(): pl.pallas_call(group_kernel, out_shape=jax.ShapeDtypeStruct((count, strea...  1.11 us
    pallas_call x1, Pallas kernels, by_group(): pl.pallas_call(unpack_kernel, out_shape=(jax.ShapeDtypeStruct((tok_rows,...  0.77 us

profile of v1, /device:TPU:0, one launch (start us, length us, event | category | flops | bytes accessed | tf_op | source)
XLA Modules:
  0.0 26.1 jit_solution(14831949209035630805)
XLA Ops:
  0.6 1.2 %pack.1 = (bf16[8,4,16,128]{3,2,1,0:T(8,128)(2,1)S(1)}, f32[1,128]{1,0:T(1,128)S(1)}) custom-call(bf16[128,128]{1,0:T(8,128)(2,1)} %query_ref.1, bf16[128,128]{1,0:T(8,128)(2,1)} %key_ref.1, bf16[128,128]{1,0:T(8,128)(2,1)} %value_ref.1, bf16[128,128]{1,0:T(8,128)(2,1)} %cot_ref.1, f32[1,128]{1,0:T(1,128)} %bitcast.2), custom_call_target="tpu_custom_call" | custom-call | tf_op jit(solution)/shard_map/pack/pallas_call | solution.py:487
  1.9 0.0 copy-start
  1.9 0.0 copy-start.1
  1.9 12.3 %all_to_all.10.in_ref = bf16[8,4,16,128]{3,2,1,0:T(8,128)(2,1)S(1)} all-to-all(bf16[8,4,16,128]{3,2,1,0:T(8,128)(2,1)S(1)} %get-tuple-element.12), channel_id=1, replica_groups={{28,24,20,16,12,8,4,0},{29,25,21,17,13,9,5,1},{30,26,22,18,14,10,6,2},{..., dimensions={0} | all-to-all | bytes 262144 | tf_op jit(solution)/shard_map/all_to_all | solution.py:509
  14.2 0.0 copy-done
  14.2 0.0 copy-done.1
  14.2 1.1 %group.1 = bf16[8,5,16,128]{3,2,1,0:T(8,128)(2,1)S(1)} custom-call(bf16[8,4,16,128]{3,2,1,0:T(8,128)(2,1)S(1)} %all_to_all.10.in_ref, f32[3,7,128]{2,1,0:T(8,128)S(1)} %copy-done.1, bf16[8,1024]{1,0:T(8,128)(2,1)S(1)} %copy-done, f32[1,128]{1,0:T(1,128)S(1)} %get-tuple-element.13.gain_ref), custom_call_target="tpu_custom_call" | custom-call | tf_op jit(solution)/shard_map/group/pallas_call | solution.py:512
  15.3 10.0 %all_to_all.11.in_ref = bf16[8,5,16,128]{3,2,1,0:T(8,128)(2,1)S(1)} all-to-all(bf16[8,5,16,128]{3,2,1,0:T(8,128)(2,1)S(1)} %group.1), channel_id=1, replica_groups={{28,24,20,16,12,8,4,0},{29,25,21,17,13,9,5,1},{30,26,22,18,14,10,6,2},{..., dimensions={0} | all-to-all | bytes 327680 | tf_op jit(solution)/shard_map/all_to_all | solution.py:525
  25.4 0.8 %unpack.1 = (bf16[128,128]{1,0:T(8,128)(2,1)}, bf16[3,128,128]{2,1,0:T(8,128)(2,1)}, f32[3,7,128]{2,1,0:T(8,128)}, f32[1,128]{1,0:T(1,128)}, f32[8,1024]{1,0:T(8,128)}) custom-call(bf16[8,5,16,128]{3,2,1,0:T(8,128)(2,1)S(1)} %all_to_all.11.in_ref), custom_call_target="tpu_custom_call" | custom-call | tf_op jit(solution)/shard_map/unpack/pallas_call | solution.py:528
Async XLA Ops:
  1.9 12.4 %copy-start = (bf16[8,1024]{1,0:T(8,128)(2,1)S(1)}, bf16[8,1024]{1,0:T(8,128)(2,1)}, u32[]{:S(2)}) copy-start(bf16[8,1024]{1,0:T(8,128)(2,1)} %filters_ref.1) | copy-start | bytes 49156
  1.9 12.3 %copy-start.1 = (f32[3,7,128]{2,1,0:T(8,128)S(1)}, f32[3,7,128]{2,1,0:T(8,128)}, u32[]{:S(2)}) copy-start(f32[3,7,128]{2,1,0:T(8,128)} %taps_ref.1) | copy-start | bytes 32260

commit v2 on v0

--- a/solution.py
+++ b/solution.py
@@ -233,6 +233,22 @@
     )
 
 
+def order_there(count):
+    return [count - 1] + list(range(count - 1))
+
+
+def order_back(count):
+    return list(range(count // 2, count)) + list(range(count // 2))
+
+
+def in_order(value, order):
+    return jnp.stack([value[order.index(device)] for device in range(len(order))])
+
+
+def by_member(value, order):
+    return jnp.stack([value[device] for device in order])
+
+
 def pack_kernel(
     query_ref, key_ref, value_ref, cot_ref, skip_ref, out_ref, gain_ref, stream_buf, sems
 ):
@@ -247,7 +263,8 @@
     for stream in range(streams):
         moves[stream].wait()
         flipped = stream_buf[stream].astype(jnp.float32).T.astype(jnp.bfloat16)
-        out_ref[:, stream] = flipped.reshape(count, members, tok_rows)
+        flipped = flipped.reshape(count, members, tok_rows)
+        out_ref[:, stream] = by_member(flipped, order_there(count))
     moves[streams].wait()
 
 
@@ -301,7 +318,8 @@
     toeplitz = jnp.concatenate(row_parts, axis=0)[:, :seq_total]
 
     def delays(stream):
-        return [later(in_ref[:, stream], first) for first in range(0, tap_count, reach)]
+        value = in_order(in_ref[:, stream], order_there(count))
+        return [later(value, first) for first in range(0, tap_count, reach)]
 
     def short(stream, values):
         total = None
@@ -323,7 +341,7 @@
         return jnp.concatenate(parts, axis=1)
 
     gain = column(streams * tap_count)
-    cot = in_ref[:, streams].astype(jnp.float32)
+    cot = in_order(in_ref[:, streams], order_there(count)).astype(jnp.float32)
     delayed = [delays(0)]
     query_short = short(0, delayed[0])
     relayed = (cot * query_short).astype(jnp.bfloat16).reshape(rows, span)
@@ -399,14 +417,15 @@
                 running = term if running is None else running + term
             running = earlier(running, reach * place)
             total = running if total is None else total + running
-        out_ref[:, 1 + stream] = total.astype(jnp.bfloat16)
+        out_ref[:, 1 + stream] = by_member(total.astype(jnp.bfloat16), order_back(count))
 
     grad_gating = backward.reshape(shape) + gain * relayed.astype(jnp.float32).reshape(shape)
     finish(1, grad_gating * value_short, reach + 1)
     finish(2, grad_gating * key_short, 2 * reach + 1)
 
     long_out = forward.reshape(shape) + gain * gating.astype(jnp.float32).reshape(shape)
-    out_ref[:, 0] = (query_short * long_out).astype(jnp.bfloat16)
+    block_out = (query_short * long_out).astype(jnp.bfloat16)
+    out_ref[:, 0] = by_member(block_out, order_back(count))
     finish(
         0, cot * long_out, 0, [tokens(relayed.reshape(shape))], [tokens(gating.reshape(shape))]
     )
@@ -428,13 +447,14 @@
     streams, tap_count, chan_width = taps_ref.shape
     reach = 3
     for stream in range(streams + 1):
-        block = in_ref[:, stream].reshape(count * members, span).astype(jnp.float32)
+        block = in_order(in_ref[:, stream], order_back(count)).reshape(count * members, span)
+        block = block.astype(jnp.float32)
         flipped = block.T.astype(jnp.bfloat16)
         if stream == 0:
             out_ref[...] = flipped
         else:
             grads_ref[stream - 1] = flipped
-    tile = in_ref[:, streams + 1].astype(jnp.float32)
+    tile = in_order(in_ref[:, streams + 1], order_back(count)).astype(jnp.float32)
     lane = lax.broadcasted_iota(jnp.int32, (1, members // 2, span), 2)
     lags = jnp.where(
         lane < span // 2, pltpu.roll(tile[:, members // 2 :], span // 2, 2), tile[:, : members // 2]
@@ -491,7 +511,9 @@
             )
         )
     )
-    packed = lax.all_to_all(packed, "seq", 0, 0, tiled=True)
+    packed = lax.all_to_all(
+        packed, "seq", 0, 0, tiled=True, axis_index_groups=[order_there(count)]
+    )
     results = pl.pallas_call(
         group_kernel,
         out_shape=jax.ShapeDtypeStruct((count, streams + 2, members, tok_rows), jnp.bfloat16),
@@ -505,7 +527,9 @@
         compiler_params=params,
         name="group",
     )(packed, short_taps, long_filters, gain)
-    results = lax.all_to_all(results, "seq", 0, 0, tiled=True)
+    results = lax.all_to_all(
+        results, "seq", 0, 0, tiled=True, axis_index_groups=[order_back(count)]
+    )
     block_out, input_grads, tap_grads, skip_grad, filter_grad = pl.pallas_call(
         unpack_kernel,
         out_shape=(

time: 28.4 us -> 26.3 us (0.926)
  blocking collectives: 24.3 us -> 22.3 us
    all_to_all x2, blocking collectives: 24.3 us -> 22.3 us  [the longest x1 12.3 us: by_group(): lax.all_to_all(packed, 'seq', 0, 0, tiled=True, axis_index_groups=[order_...]
where the time goes in v2:
time: 26.3 us; the launch traced here: 26 us
  blocking collectives  22.3 us (85%)
  Pallas kernels  3.1 us (12%)
  between operations  0.66 us (3%)
    all_to_all x1, blocking collectives, by_group(): lax.all_to_all(packed, 'seq', 0, 0, tiled=True, axis_index_groups=[order_...  12.3 us
    all_to_all x1, blocking collectives, by_group(): lax.all_to_all(results, 'seq', 0, 0, tiled=True, axis_index_groups=[order...  9.91 us
    pallas_call x1, Pallas kernels, by_group(): pl.pallas_call(pack_kernel, out_shape=(jax.ShapeDtypeStruct((count, strea...  1.22 us
    pallas_call x1, Pallas kernels, by_group(): pl.pallas_call(group_kernel, out_shape=jax.ShapeDtypeStruct((count, strea...  1.11 us
    pallas_call x1, Pallas kernels, by_group(): pl.pallas_call(unpack_kernel, out_shape=(jax.ShapeDtypeStruct((tok_rows,...  0.77 us

profile of v2, /device:TPU:0, one launch (start us, length us, event | category | flops | bytes accessed | tf_op | source)
XLA Modules:
  0.0 26.0 jit_solution(9896466022017485545)
XLA Ops:
  0.6 1.2 %pack.1 = (bf16[8,4,16,128]{3,2,1,0:T(8,128)(2,1)S(1)}, f32[1,128]{1,0:T(1,128)S(1)}) custom-call(bf16[128,128]{1,0:T(8,128)(2,1)} %query_ref.1, bf16[128,128]{1,0:T(8,128)(2,1)} %key_ref.1, bf16[128,128]{1,0:T(8,128)(2,1)} %value_ref.1, bf16[128,128]{1,0:T(8,128)(2,1)} %cot_ref.1, f32[1,128]{1,0:T(1,128)} %bitcast.2), custom_call_target="tpu_custom_call" | custom-call | tf_op jit(solution)/shard_map/pack/pallas_call | solution.py:492
  1.9 0.0 copy-start
  1.9 0.0 copy-start.1
  1.9 12.3 %all_to_all.10.in_ref = bf16[8,4,16,128]{3,2,1,0:T(8,128)(2,1)S(1)} all-to-all(bf16[8,4,16,128]{3,2,1,0:T(8,128)(2,1)S(1)} %get-tuple-element.12), channel_id=1, replica_groups={{28,0,4,8,12,16,20,24},{29,1,5,9,13,17,21,25},{30,2,6,10,14,18,22,26},{..., dimensions={0} | all-to-all | bytes 262144 | tf_op jit(solution)/shard_map/all_to_all | solution.py:514
  14.2 0.0 copy-done
  14.2 0.0 copy-done.1
  14.2 1.1 %group.1 = bf16[8,5,16,128]{3,2,1,0:T(8,128)(2,1)S(1)} custom-call(bf16[8,4,16,128]{3,2,1,0:T(8,128)(2,1)S(1)} %all_to_all.10.in_ref, f32[3,7,128]{2,1,0:T(8,128)S(1)} %copy-done.1, bf16[8,1024]{1,0:T(8,128)(2,1)S(1)} %copy-done, f32[1,128]{1,0:T(1,128)S(1)} %get-tuple-element.13.gain_ref), custom_call_target="tpu_custom_call" | custom-call | tf_op jit(solution)/shard_map/group/pallas_call | solution.py:517
  15.3 9.9 %all_to_all.11.in_ref = bf16[8,5,16,128]{3,2,1,0:T(8,128)(2,1)S(1)} all-to-all(bf16[8,5,16,128]{3,2,1,0:T(8,128)(2,1)S(1)} %group.1), channel_id=1, replica_groups={{16,20,24,28,0,4,8,12},{17,21,25,29,1,5,9,13},{18,22,26,30,2,6,10,14},{..., dimensions={0} | all-to-all | bytes 327680 | tf_op jit(solution)/shard_map/all_to_all | solution.py:530
  25.3 0.8 %unpack.1 = (bf16[128,128]{1,0:T(8,128)(2,1)}, bf16[3,128,128]{2,1,0:T(8,128)(2,1)}, f32[3,7,128]{2,1,0:T(8,128)}, f32[1,128]{1,0:T(1,128)}, f32[8,1024]{1,0:T(8,128)}) custom-call(bf16[8,5,16,128]{3,2,1,0:T(8,128)(2,1)S(1)} %all_to_all.11.in_ref), custom_call_target="tpu_custom_call" | custom-call | tf_op jit(solution)/shard_map/unpack/pallas_call | solution.py:533
Async XLA Ops:
  1.9 12.4 %copy-start = (bf16[8,1024]{1,0:T(8,128)(2,1)S(1)}, bf16[8,1024]{1,0:T(8,128)(2,1)}, u32[]{:S(2)}) copy-start(bf16[8,1024]{1,0:T(8,128)(2,1)} %filters_ref.1) | copy-start | bytes 49156
  1.9 12.4 %copy-start.1 = (f32[3,7,128]{2,1,0:T(8,128)S(1)}, f32[3,7,128]{2,1,0:T(8,128)}, u32[]{:S(2)}) copy-start(f32[3,7,128]{2,1,0:T(8,128)} %taps_ref.1) | copy-start | bytes 32260

commit v3 on v2

--- a/solution.py
+++ b/solution.py
@@ -234,11 +234,11 @@
 
 
 def order_there(count):
-    return [count - 1] + list(range(count - 1))
+    return list(range(count // 2 + 1, count)) + list(range(count // 2 + 1))
 
 
 def order_back(count):
-    return list(range(count // 2, count)) + list(range(count // 2))
+    return list(range(count // 2 + 1, count)) + list(range(count // 2 + 1))
 
 
 def in_order(value, order):

time: 26.3 us -> 25 us (0.951)
  blocking collectives: 22.3 us -> 20.9 us
    all_to_all x1, blocking collectives: 9.91 us -> 9.19 us  [by_group(): lax.all_to_all(results, 'seq', 0, 0, tiled=True, axis_index_groups=[order...]
    all_to_all x1, blocking collectives: 12.3 us -> 11.7 us  [by_group(): lax.all_to_all(packed, 'seq', 0, 0, tiled=True, axis_index_groups=[order_...]
where the time goes in v3:
time: 25 us; the launch traced here: 24.7 us
  blocking collectives  20.9 us (84%)
  Pallas kernels  3.1 us (12%)
  between operations  0.66 us (3%)
    all_to_all x1, blocking collectives, by_group(): lax.all_to_all(packed, 'seq', 0, 0, tiled=True, axis_index_groups=[order_...  11.7 us
    all_to_all x1, blocking collectives, by_group(): lax.all_to_all(results, 'seq', 0, 0, tiled=True, axis_index_groups=[order...  9.19 us
    pallas_call x1, Pallas kernels, by_group(): pl.pallas_call(pack_kernel, out_shape=(jax.ShapeDtypeStruct((count, strea...  1.22 us
    pallas_call x1, Pallas kernels, by_group(): pl.pallas_call(group_kernel, out_shape=jax.ShapeDtypeStruct((count, strea...  1.11 us
    pallas_call x1, Pallas kernels, by_group(): pl.pallas_call(unpack_kernel, out_shape=(jax.ShapeDtypeStruct((tok_rows,...  0.77 us

profile of v3, /device:TPU:0, one launch (start us, length us, event | category | flops | bytes accessed | tf_op | source)
XLA Modules:
  0.0 24.7 jit_solution(10708737565451150012)
XLA Ops:
  0.6 1.2 %pack.1 = (bf16[8,4,16,128]{3,2,1,0:T(8,128)(2,1)S(1)}, f32[1,128]{1,0:T(1,128)S(1)}) custom-call(bf16[128,128]{1,0:T(8,128)(2,1)} %query_ref.1, bf16[128,128]{1,0:T(8,128)(2,1)} %key_ref.1, bf16[128,128]{1,0:T(8,128)(2,1)} %value_ref.1, bf16[128,128]{1,0:T(8,128)(2,1)} %cot_ref.1, f32[1,128]{1,0:T(1,128)} %bitcast.2), custom_call_target="tpu_custom_call" | custom-call | tf_op jit(solution)/shard_map/pack/pallas_call | solution.py:492
  1.9 0.0 copy-start
  1.9 0.0 copy-start.1
  1.9 11.7 %all_to_all.10.in_ref = bf16[8,4,16,128]{3,2,1,0:T(8,128)(2,1)S(1)} all-to-all(bf16[8,4,16,128]{3,2,1,0:T(8,128)(2,1)S(1)} %get-tuple-element.12), channel_id=1, replica_groups={{20,24,28,0,4,8,12,16},{21,25,29,1,5,9,13,17},{22,26,30,2,6,10,14,18},{..., dimensions={0} | all-to-all | bytes 262144 | tf_op jit(solution)/shard_map/all_to_all | solution.py:514
  13.6 0.0 copy-done
  13.6 0.0 copy-done.1
  13.6 1.1 %group.1 = bf16[8,5,16,128]{3,2,1,0:T(8,128)(2,1)S(1)} custom-call(bf16[8,4,16,128]{3,2,1,0:T(8,128)(2,1)S(1)} %all_to_all.10.in_ref, f32[3,7,128]{2,1,0:T(8,128)S(1)} %copy-done.1, bf16[8,1024]{1,0:T(8,128)(2,1)S(1)} %copy-done, f32[1,128]{1,0:T(1,128)S(1)} %get-tuple-element.13.gain_ref), custom_call_target="tpu_custom_call" | custom-call | tf_op jit(solution)/shard_map/group/pallas_call | solution.py:517
  14.7 9.2 %all_to_all.11.in_ref = bf16[8,5,16,128]{3,2,1,0:T(8,128)(2,1)S(1)} all-to-all(bf16[8,5,16,128]{3,2,1,0:T(8,128)(2,1)S(1)} %group.1), channel_id=1, replica_groups={{20,24,28,0,4,8,12,16},{21,25,29,1,5,9,13,17},{22,26,30,2,6,10,14,18},{..., dimensions={0} | all-to-all | bytes 327680 | tf_op jit(solution)/shard_map/all_to_all | solution.py:530
  23.9 0.8 %unpack.1 = (bf16[128,128]{1,0:T(8,128)(2,1)}, bf16[3,128,128]{2,1,0:T(8,128)(2,1)}, f32[3,7,128]{2,1,0:T(8,128)}, f32[1,128]{1,0:T(1,128)}, f32[8,1024]{1,0:T(8,128)}) custom-call(bf16[8,5,16,128]{3,2,1,0:T(8,128)(2,1)S(1)} %all_to_all.11.in_ref), custom_call_target="tpu_custom_call" | custom-call | tf_op jit(solution)/shard_map/unpack/pallas_call | solution.py:533
Async XLA Ops:
  1.9 11.7 %copy-start = (bf16[8,1024]{1,0:T(8,128)(2,1)S(1)}, bf16[8,1024]{1,0:T(8,128)(2,1)}, u32[]{:S(2)}) copy-start(bf16[8,1024]{1,0:T(8,128)(2,1)} %filters_ref.1) | copy-start | bytes 49156
  1.9 11.7 %copy-start.1 = (f32[3,7,128]{2,1,0:T(8,128)S(1)}, f32[3,7,128]{2,1,0:T(8,128)}, u32[]{:S(2)}) copy-start(f32[3,7,128]{2,1,0:T(8,128)} %taps_ref.1) | copy-start | bytes 32260
